TPU v7x, 32 devices: a whole 2x2x4 slice. The times are simulated.
32 devices in a mesh: groups: 2 (over y), train: 4 (over z), mat: 2 (over x), sub: 2 (over core).
Axes of the slice: x: 2, y: 2, z: 4, core: 2. Of those that a mesh axis runs over, the one named last changes fastest.
Arguments:
- train_grads: bfloat16 [2048, 8, 4096], P(('groups', 'train'), 'mat'), parts along dimension 0, may hold values from -6 to 6
- test_grads: bfloat16 [4, 56, 8, 4096], P(('groups', 'sub'), 'train', 'mat'), parts along dimension 0, may hold values from -0.03125 to 0.03125
- slab_counts: int32 [8], P(('groups', 'train')), parts along dimension 0, may hold values from 64 to 256, as said below
- test_order: int32 [4, 56], P(('groups', 'sub')), parts along dimension 0, may hold values from 0 to 55, each once within a row
Outputs:
- scores: float32 [2048, 2, 56], P(('groups', 'train', 'mat'), 'sub'), parts along dimension 0
There are 2 independent parts, one for each index of `groups`. A program takes and returns all parts, laid end to end along the dimension named above; each array names one. Nothing has to cross between parts.
Inputs may be any that keep to these rules, and one draw needn't show every extreme that they name: `slab_counts`: each slab block holds between 64 and 256 live rows; some block is full and some holds exactly 64. Each row of test_order is a permutation of 0 to 55.
All inputs are finite; a program needn't handle non-finite values.
Results may differ from a plain program's by a relative error of at most 0.0003.
Values may be sent and summed in bfloat16 or wider, within the bound.
A program may use at most 128 MiB of HBM per device.

v0:
```python
import jax
import jax.numpy as jnp
from jax import lax
from jax.sharding import PartitionSpec as P


def shards(train_grads, test_grads, slab_counts, test_order):
    rows_dev = train_grads.shape[0]
    mat_count = lax.axis_size("mat")
    sub_count = lax.axis_size("sub")
    quarter = rows_dev // mat_count
    feature_count = train_grads.shape[1] * train_grads.shape[2]
    test_rows = lax.all_gather(test_grads, "sub", axis=0, tiled=True)
    share_rows = quarter // sub_count
    grouped = train_grads.reshape(mat_count, sub_count, share_rows, feature_count)
    local_rows = lax.dynamic_index_in_dim(grouped, lax.axis_index("sub"), 1, keepdims=False)
    local_rows = local_rows.reshape(mat_count * share_rows, feature_count)
    live_count = slab_counts[0]
    local_total = local_rows.shape[0]
    halves = test_rows.shape[0]
    incoming = lax.all_gather(test_rows, "train", axis=1, tiled=True)
    width_now = incoming.shape[1]
    flat_piece = incoming.reshape(halves * width_now, feature_count)
    product = lax.dot_general(
        local_rows, flat_piece, (((1,), (1,)), ((), ())), preferred_element_type=jnp.float32
    )
    scores = product.reshape(local_total, halves, width_now)
    summed = lax.psum_scatter(scores, "mat", scatter_dimension=0, tiled=True)
    summed = lax.all_to_all(summed, "sub", split_axis=1, concat_axis=0, tiled=True)
    out_positions = lax.axis_index("mat") * quarter + jnp.arange(quarter, dtype=jnp.int32)
    masked = jnp.where((out_positions < live_count)[:, None], summed[:, 0, :], jnp.float32(0.0))
    return masked[:, test_order[0]][:, None, :]


def solution(mesh):
    placed = (
        P(("groups", "train"), "mat", None),
        P(("groups", "sub"), "train", "mat", None),
        P(("groups", "train")),
        P(("groups", "sub"), None),
    )
    return jax.shard_map(
        shards,
        mesh=mesh,
        in_specs=placed,
        out_specs=P(("groups", "train", "mat"), "sub", None),
        check_vma=False,
    )
```

profile of v0, /device:TPU:0, one launch (start us, length us, event | category | flops | bytes accessed | tf_op | source)
XLA Modules:
  0.0 123.7 jit_solution(17622311856808133724)
XLA Ops:
  6.5 0.0 all-gather.2.cloned.1.call-start
  6.5 7.1 %all_gather.6 = bf16[2,14,4,4096]{3,2,1,0:T(4,128)(2,1)} all-gather(bf16[1,14,4,4096]{3,2,1,0:T(4,128)(2,1)} %param.5), channel_id=1, replica_groups=mesh['groups'=2,'train'=4,'mat'=2,'sub'=2] {'sub'}, dimensions={0}, use_global_device_ids=true | all-gather | bytes 1376256 | tf_op jit(solution)/shard_map/all_gather | solution.py:13
  13.7 0.0 all-gather.2.cloned.1.call-update
  13.7 0.0 reduce-scatter.4.cloned.1.call-start
  13.8 0.0 copy-start
  13.8 14.5 %reshape.45 = bf16[2,2,64,16384]{3,2,1,0:T(8,128)(2,1)} reshape(bf16[256,4,4096]{2,1,0:T(4,128)(2,1)} %param.4) | data formatting | bytes 16777216 | tf_op jit(solution)/shard_map/reshape | solution.py:15
  29.0 0.0 copy-done
  29.0 4.5 %constant_dynamic-slice_fusion = bf16[2,1,64,16384]{3,2,1,0:T(8,128)(2,1)} fusion(bf16[2,2,64,16384]{3,2,1,0:T(8,128)(2,1)} %reshape.45, s32[]{:T(128)S(6)} %select_n.18), kind=kLoop, calls=%fused_computation.6 | loop fusion | bytes 8388612 | tf_op jit(solution)/shard_map/jit(dynamic_index_in_dim)/dynamic_slice | solution.py:16
  33.5 54.9 %all-gather.2.cloned.1.call-done = bf16[2,56,4,4096]{3,2,1,0:T(4,128)(2,1)} async-done(((bf16[2,14,4,4096]{3,2,1,0:T(4,128)(2,1)}), bf16[2,56,4,4096]{3,2,1,0:T(4,128)(2,1)}) %all-gather.2.cloned.1.call-update) | async-done | bytes 3670032 | tf_op jit(solution)/shard_map/all_gather | solution.py:21
  88.4 7.1 %dot_general.5 = bf16[2,56,16384]{2,1,0:T(8,128)(2,1)} reshape(bf16[2,56,4,4096]{3,2,1,0:T(4,128)(2,1)} %all-gather.2.cloned.1.call-done) | data formatting | bytes 7340032 | tf_op jit(solution)/shard_map/dot_general | solution.py:24
  95.5 4.6 %fusion.1 = f32[128,2,56]{0,2,1:T(8,128)S(1)} fusion(bf16[128,16384,1]{1,0,2:T(8,128)(2,1)} %bitcast.28, bf16[2,56,16384]{2,1,0:T(8,128)(2,1)} %dot_general.5), kind=kOutput, calls=%fused_computation.8 | convolution fusion | flops 469762048 | bytes 7921664 | tf_op jit(solution)/shard_map/dot_general | solution.py:24
  100.1 0.7 copy.12
  100.8 0.0 reduce-scatter.4.cloned.1.call-update
  100.9 8.6 %reduce-scatter.4.cloned.1.call-done = f32[64,112]{1,0:T(8,128)} async-done(((f32[128,112]{1,0:T(8,128)}), f32[64,112]{1,0:T(8,128)}) %reduce-scatter.4.cloned.1.call-update) | async-done | bytes 28688
  109.5 0.8 copy.13
  110.3 0.1 reshape.58
  110.4 3.7 %all_to_all.15 = f32[2,1,3584]{2,1,0:T(1,128)S(1)} all-to-all(f32[2,1,3584]{2,1,0:T(1,128)S(1)} %reshape.58), channel_id=1, replica_groups=mesh['groups'=2,'train'=4,'mat'=2,'sub'=2] {'sub'}, dimensions={0} | all-to-all | bytes 57344 | tf_op jit(solution)/shard_map/all_to_all | solution.py:29
  114.2 0.5 broadcast.26
  114.7 0.7 reduce
  115.4 0.1 reshape.59
  115.5 0.1 squeeze.12
  115.7 1.2 gather_fusion
  (6 shorter events, 0.1 us)
Async XLA Ops:
  6.5 81.9 %all-gather.2.cloned.1.call-start = ((), (), s32[]{:S(2)}) async-start(), calls=%async_computation.2 | async-start | bytes 4587520 | tf_op jit(solution)/shard_map/all_gather | solution.py:21
  13.7 95.8 %reduce-scatter.4.cloned.1.call-start = ((), (), s32[]{:S(2)}) async-start(), calls=%async_computation.3 | async-start | bytes 98304
  13.8 15.2 %copy-start = (s32[1,56]{1,0:T(1,128)S(1)}, s32[1,56]{1,0:T(1,128)}, u32[]{:S(2)}) copy-start(s32[1,56]{1,0:T(1,128)} %param.7) | copy-start | bytes 676
Sparse Core Ops, SparseCore 0:
  13.8 74.5 all-gather.1
  101.0 8.4 reduce-scatter.3
where the time goes:
time: 125 us; the launch traced here: 124 us
  waiting for transfers between devices  63.5 us (51%)
  local copies, waits for them, and re-layouts  29.8 us (24%)
  between operations  14.1 us (11%)
  blocking collectives  10.9 us (9%)
  matrix products  4.58 us (4%)
    all_gather x1, waiting for transfers between devices, shards(): incoming = lax.all_gather(test_rows, 'train', axis=1, tiled=True)  54.9 us
    reshape x1, local copies, waits for them, and re-layouts, shards(): train_grads.reshape(mat_count, sub_count, share_rows, feature_count)  14.5 us
    unnamed x3, waiting for transfers between devices  8.65 us
    all_gather x1, blocking collectives, shards(): test_rows = lax.all_gather(test_grads, 'sub', axis=0, tiled=True)  7.13 us
    dot_general x1, local copies, waits for them, and re-layouts, shards(): lax.dot_general(local_rows, flat_piece, (((1,), (1,)), ((), ())), preferr...  7.11 us
    dot_general x1, matrix products, shards(): lax.dot_general(local_rows, flat_piece, (((1,), (1,)), ((), ())), preferr...  4.58 us
    dynamic_slice x1, local copies, waits for them, and re-layouts, shards(): lax.dynamic_index_in_dim(grouped, lax.axis_index('sub'), 1, keepdims=False)  4.53 us
    all_to_all x1, blocking collectives, shards(): lax.all_to_all(summed, 'sub', split_axis=1, concat_axis=0, tiled=True)  3.74 us
  transfers between devices with their start and end apart: 2, of which 2 were waited for; matrix products, arithmetic and copies ran while one was open for 15% of the time, Pallas kernels for 0%

commit v1 on v0

v1 whole, which is shorter than its diff:
```python
import functools

import jax
import jax.numpy as jnp
from jax import lax
from jax.experimental import pallas as pl
from jax.experimental.pallas import tpu as pltpu
from jax.sharding import PartitionSpec as P

MESH = pl.DeviceIdType.MESH


def kernel(
    n,
    mat_count,
    pieces,
    train_ref,
    test_ref,
    count_ref,
    order_ref,
    out_ref,
    train_in,
    rows_mat,
    tests,
    total,
    outgoing,
    incoming,
    send_sem,
    recv_sem,
    load_sem,
    own_sem,
    out_sem,
    in_sem,
):
    z = lax.axis_index("train")
    mat = lax.axis_index("mat")
    rows, mats, features = train_ref.shape
    held = test_ref.shape[1]
    width = features // pieces
    quarter = rows // mat_count
    columns = out_ref.shape[0]

    barrier = pltpu.get_barrier_semaphore()

    @pl.when(z > 0)
    def _():
        pl.semaphore_signal(barrier, inc=1, device_id={"train": z - 1}, device_id_type=MESH)

    @pl.when(z < n - 1)
    def _():
        pl.semaphore_signal(barrier, inc=1, device_id={"train": z + 1}, device_id_type=MESH)

    for j in range(1, mat_count):
        pl.semaphore_signal(
            barrier, inc=1, device_id={"mat": lax.rem(mat + j, mat_count)}, device_id_type=MESH
        )

    def span(k):
        return pl.ds(pl.multiple_of(k * width, width), width)

    def load_own(k):
        return pltpu.make_async_copy(
            test_ref.at[0, :, :, span(k)], tests.at[z, :, :, span(k)], own_sem.at[k]
        )

    def load_train(k):
        return pltpu.make_async_copy(
            train_ref.at[:, :, span(k)], train_in.at[:, :, span(k)], load_sem.at[k]
        )

    for k in range(pieces):
        load_own(k).start()
        load_train(k).start()

    neighbours = (z > 0).astype(jnp.int32) + (z < n - 1).astype(jnp.int32)
    pl.semaphore_wait(barrier, neighbours + (mat_count - 1))

    def pass_on(src, chunk, k, side):
        return pltpu.make_async_remote_copy(
            src_ref=src,
            dst_ref=tests.at[chunk, :, :, span(k)],
            send_sem=send_sem.at[chunk, side, k],
            recv_sem=recv_sem.at[chunk, k],
            device_id={"train": z - 1 if side == 0 else z + 1},
            device_id_type=MESH,
        )

    def from_own(k, side):
        return pass_on(test_ref.at[0, :, :, span(k)], z, k, side)

    def from_held(chunk, k, side):
        return pass_on(tests.at[chunk, :, :, span(k)], chunk, k, side)

    for k in range(pieces):
        @pl.when(z > 0)
        def _():
            from_own(k, 0).start()

        @pl.when(z < n - 1)
        def _():
            from_own(k, 1).start()

    def close_chunk(chunk, slot, first):
        column_mat = lax.broadcasted_iota(jnp.int32, (rows, held * mats), 1) % mats
        summed = jnp.zeros((rows, held * mats), jnp.float32)
        for m in range(mats):
            strided = slot[pl.ds(m, rows, stride=mats), :]
            summed += jnp.where(column_mat == m, strided, 0.0)
        source = chunk * held + lax.broadcasted_iota(jnp.int32, (held * mats, columns), 0) // mats
        pick = jnp.where(source == order_ref[...], 1.0, 0.0).T
        for j in range(mat_count):
            moved = lax.dot_general(
                pick,
                summed[j * quarter : (j + 1) * quarter],
                (((1,), (1,)), ((), ())),
                precision=lax.Precision.HIGHEST,
                preferred_element_type=jnp.float32,
            )
            if first:
                outgoing[j] = moved
            else:
                outgoing[j] += moved

    left_total, right_total = total.at[0], total.at[1]

    def add(slot, chunk, k):
        block = tests[chunk, :, :, span(k)].reshape(held * mats, width)
        part = lax.dot_general(
            rows_mat[:, span(k)],
            block,
            (((1,), (1,)), ((), ())),
            preferred_element_type=jnp.float32,
        )
        slot[...] = jnp.where(k == 0, 0.0, slot[...]) + part

    def own_piece(k, carry):
        load_train(k).wait()
        rows_mat[:, span(k)] = train_in[:, :, span(k)].reshape(rows * mats, width)
        load_own(k).wait()
        add(left_total, z, k)
        return carry

    lax.fori_loop(0, pieces, own_piece, 0)
    close_chunk(z, left_total, True)

    def hop(d, carry):
        low, high = z - d, z + d

        def piece(k, carry):
            @pl.when(low >= 0)
            def _():
                from_held(low, k, 1).wait_recv()

                @pl.when(z < n - 1)
                def _():
                    from_held(low, k, 1).start()

            @pl.when(high < n)
            def _():
                from_held(high, k, 0).wait_recv()

                @pl.when(z > 0)
                def _():
                    from_held(high, k, 0).start()

            @pl.when(low >= 0)
            def _():
                add(left_total, low, k)

            @pl.when(high < n)
            def _():
                add(right_total, high, k)

            return carry

        lax.fori_loop(0, pieces, piece, 0)

        @pl.when(low >= 0)
        def _():
            close_chunk(low, left_total, False)

        @pl.when(high < n)
        def _():
            close_chunk(high, right_total, False)

        return carry

    lax.fori_loop(1, n, hop, 0)

    def swap(j):
        other = lax.rem(mat + j, mat_count)
        return pltpu.make_async_remote_copy(
            src_ref=outgoing.at[other],
            dst_ref=incoming.at[j],
            send_sem=out_sem.at[j],
            recv_sem=in_sem.at[j],
            device_id={"mat": other},
            device_id_type=MESH,
        )

    for j in range(1, mat_count):
        swap(j).start()
    score = outgoing[mat]
    for j in range(1, mat_count):
        swap(j).wait()
        score += incoming[j]
    place = mat * quarter + lax.broadcasted_iota(jnp.int32, (columns, quarter), 1)
    out_ref[...] = jnp.where(place < count_ref[0], score, 0.0)

    def drain(k, carry):
        @pl.when(z > 0)
        def _():
            from_own(k, 0).wait_send()

        @pl.when(z < n - 1)
        def _():
            from_own(k, 1).wait_send()

        def drain_hop(d, carry):
            @pl.when((z - d >= 0) & (z < n - 1))
            def _():
                from_held(z - d, k, 1).wait_send()

            @pl.when((z + d < n) & (z > 0))
            def _():
                from_held(z + d, k, 0).wait_send()

            return carry

        return lax.fori_loop(1, n, drain_hop, carry)

    lax.fori_loop(0, pieces, drain, 0)


def solution(mesh):
    n = mesh.shape["train"]
    mat_count = mesh.shape["mat"]
    pieces = 4

    def shards(train_grads, test_grads, slab_counts, test_order):
        rows, mats, features = train_grads.shape
        held = test_grads.shape[1]
        columns = test_order.shape[1]
        quarter = rows // mat_count
        any_space = pl.BlockSpec(memory_space=pl.ANY)
        found = pl.pallas_call(
            functools.partial(kernel, n, mat_count, pieces),
            out_shape=jax.ShapeDtypeStruct((columns, quarter), jnp.float32),
            in_specs=[
                any_space,
                any_space,
                pl.BlockSpec(memory_space=pltpu.SMEM),
                pl.BlockSpec(memory_space=pltpu.VMEM),
            ],
            out_specs=pl.BlockSpec(memory_space=pltpu.VMEM),
            scratch_shapes=[
                pltpu.VMEM((rows, mats, features), jnp.bfloat16),
                pltpu.VMEM((rows * mats, features), jnp.bfloat16),
                pltpu.VMEM((n, held, mats, features), jnp.bfloat16),
                pltpu.VMEM((2, rows * mats, held * mats), jnp.float32),
                pltpu.VMEM((mat_count, columns, quarter), jnp.float32),
                pltpu.VMEM((mat_count, columns, quarter), jnp.float32),
                pltpu.SemaphoreType.DMA((n, 2, pieces)),
                pltpu.SemaphoreType.DMA((n, pieces)),
                pltpu.SemaphoreType.DMA((pieces,)),
                pltpu.SemaphoreType.DMA((pieces,)),
                pltpu.SemaphoreType.DMA((mat_count,)),
                pltpu.SemaphoreType.DMA((mat_count,)),
            ],
            compiler_params=pltpu.CompilerParams(
                collective_id=0, has_side_effects=True, vmem_limit_bytes=56 * 1024 * 1024
            ),
        )(train_grads, test_grads, slab_counts, test_order)
        return found.T[:, None, :]

    placed = (
        P(("groups", "train"), "mat", None),
        P(("groups", "sub"), "train", "mat", None),
        P(("groups", "train")),
        P(("groups", "sub"), None),
    )
    return jax.shard_map(
        shards,
        mesh=mesh,
        in_specs=placed,
        out_specs=P(("groups", "train", "mat"), "sub", None),
        check_vma=False,
    )
```

time: 125 us -> 43.2 us (0.35)
  waiting for transfers between devices: 63.5 us -> 0 us
  Pallas kernels: 0 us -> 41 us
  local copies, waits for them, and re-layouts: 29.8 us -> 1.36 us
  between operations: 14.1 us -> 0.66 us
  blocking collectives: 10.9 us -> 0 us
  matrix products: 4.58 us -> 0 us
    all_gather x1 -> x0, waiting for transfers between devices: 54.9 us -> none  [shards(): incoming = lax.all_gather(test_rows, 'train', axis=1, tiled=True)]
    pallas_call x0 -> x1, Pallas kernels: none -> 41 us  [shards(): pl.pallas_call(functools.partial(kernel, n, mat_count, pieces), out_shape...]
    reshape x1 -> x0, local copies, waits for them, and re-layouts: 14.5 us -> none  [shards(): train_grads.reshape(mat_count, sub_count, share_rows, feature_count)]
    unnamed x3 -> x0, waiting for transfers between devices: 8.65 us -> none
    all_gather x1 -> x0, blocking collectives: 7.13 us -> none  [shards(): test_rows = lax.all_gather(test_grads, 'sub', axis=0, tiled=True)]
    dot_general x1 -> x0, local copies, waits for them, and re-layouts: 7.11 us -> none  [shards(): lax.dot_general(local_rows, flat_piece, (((1,), (1,)), ((), ())), preferr...]
    dot_general x1 -> x0, matrix products: 4.58 us -> none  [shards(): lax.dot_general(local_rows, flat_piece, (((1,), (1,)), ((), ())), preferr...]
    dynamic_slice x1 -> x0, local copies, waits for them, and re-layouts: 4.53 us -> none  [shards(): lax.dynamic_index_in_dim(grouped, lax.axis_index('sub'), 1, keepdims=False)]
  transfers between devices with their start and end apart: 2 -> 0, of which waited for: 2 -> 0; matrix products, arithmetic and copies ran while one was open for 15% -> 0% of each run, Pallas kernels for 0% -> 0%
where the time goes in v1:
time: 43.2 us; the launch traced here: 43 us
  Pallas kernels  41 us (95%)
  local copies, waits for them, and re-layouts  1.36 us (3%)
  between operations  0.66 us (2%)
    pallas_call x1, Pallas kernels, shards(): pl.pallas_call(functools.partial(kernel, n, mat_count, pieces), out_shape...  41 us
    unnamed x1, local copies, waits for them, and re-layouts  1.36 us

profile of v1, /device:TPU:0, one launch (start us, length us, event | category | flops | bytes accessed | tf_op | source)
XLA Modules:
  0.0 43.0 jit_solution(1301769077472510834)
XLA Ops:
  0.7 41.0 %shard_map.46 = f32[56,128]{1,0:T(8,128)} custom-call(bf16[256,4,4096]{2,1,0:T(4,128)(2,1)} %train_ref.1, bf16[1,14,4,4096]{3,2,1,0:T(4,128)(2,1)} %test_ref.1, s32[1]{0:T(128)S(6)} %copy.6.count_ref, s32[1,56]{1,0:T(1,128)} %order_ref.1), custom_call_target="tpu_custom_call" | custom-call | tf_op jit(solution)/shard_map/pallas_call | solution.py:246
  41.7 1.4 %copy.7 = f32[128,1,56]{0,2,1:T(8,128)} copy(f32[128,1,56]{0,2,1:T(8,128)} %bitcast.3) | data formatting | bytes 57344

commit v2 on v1

--- a/solution.py
+++ b/solution.py
@@ -92,11 +92,20 @@
         return pass_on(tests.at[chunk, :, :, span(k)], chunk, k, side)
 
     for k in range(pieces):
-        @pl.when(z > 0)
+        @pl.when((z > 0) & (z < n - 1 - z))
         def _():
             from_own(k, 0).start()
 
-        @pl.when(z < n - 1)
+        @pl.when((z < n - 1) & (z >= n - 1 - z))
+        def _():
+            from_own(k, 1).start()
+
+    for k in range(pieces):
+        @pl.when((z > 0) & (z >= n - 1 - z))
+        def _():
+            from_own(k, 0).start()
+
+        @pl.when((z < n - 1) & (z < n - 1 - z))
         def _():
             from_own(k, 1).start()
 
@@ -121,7 +130,7 @@
             else:
                 outgoing[j] += moved
 
-    left_total, right_total = total.at[0], total.at[1]
+    left_total, right_total, own_total = total.at[0], total.at[1], total.at[2]
 
     def add(slot, chunk, k):
         block = tests[chunk, :, :, span(k)].reshape(held * mats, width)
@@ -133,15 +142,13 @@
         )
         slot[...] = jnp.where(k == 0, 0.0, slot[...]) + part
 
-    def own_piece(k, carry):
+    def own_piece(k):
         load_train(k).wait()
         rows_mat[:, span(k)] = train_in[:, :, span(k)].reshape(rows * mats, width)
         load_own(k).wait()
-        add(left_total, z, k)
-        return carry
-
-    lax.fori_loop(0, pieces, own_piece, 0)
-    close_chunk(z, left_total, True)
+        add(own_total, z, k)
+
+    outgoing[...] = jnp.zeros_like(outgoing)
 
     def hop(d, carry):
         low, high = z - d, z + d
@@ -163,6 +170,10 @@
                 def _():
                     from_held(high, k, 0).start()
 
+            @pl.when(d == 1)
+            def _():
+                own_piece(k)
+
             @pl.when(low >= 0)
             def _():
                 add(left_total, low, k)
@@ -174,6 +185,10 @@
             return carry
 
         lax.fori_loop(0, pieces, piece, 0)
+
+        @pl.when(d == 1)
+        def _():
+            close_chunk(z, own_total, False)
 
         @pl.when(low >= 0)
         def _():
@@ -257,7 +272,7 @@
                 pltpu.VMEM((rows, mats, features), jnp.bfloat16),
                 pltpu.VMEM((rows * mats, features), jnp.bfloat16),
                 pltpu.VMEM((n, held, mats, features), jnp.bfloat16),
-                pltpu.VMEM((2, rows * mats, held * mats), jnp.float32),
+                pltpu.VMEM((3, rows * mats, held * mats), jnp.float32),
                 pltpu.VMEM((mat_count, columns, quarter), jnp.float32),
                 pltpu.VMEM((mat_count, columns, quarter), jnp.float32),
                 pltpu.SemaphoreType.DMA((n, 2, pieces)),

time: 43.2 us -> 43.2 us (level)
  no operation moved by 1% of the time
where the time goes in v2:
time: 43.2 us; the launch traced here: 43.1 us
  Pallas kernels  41 us (95%)
  local copies, waits for them, and re-layouts  1.36 us (3%)
  between operations  0.66 us (2%)
    pallas_call x1, Pallas kernels, shards(): pl.pallas_call(functools.partial(kernel, n, mat_count, pieces), out_shape...  41 us
    unnamed x1, local copies, waits for them, and re-layouts  1.36 us

profile of v2, /device:TPU:0, one launch (start us, length us, event | category | flops | bytes accessed | tf_op | source)
XLA Modules:
  0.0 43.1 jit_solution(1748091951958814413)
XLA Ops:
  0.7 41.0 %shard_map.46 = f32[56,128]{1,0:T(8,128)} custom-call(bf16[256,4,4096]{2,1,0:T(4,128)(2,1)} %train_ref.1, bf16[1,14,4,4096]{3,2,1,0:T(4,128)(2,1)} %test_ref.1, s32[1]{0:T(128)S(6)} %copy.6.count_ref, s32[1,56]{1,0:T(1,128)} %order_ref.1), custom_call_target="tpu_custom_call" | custom-call | tf_op jit(solution)/shard_map/pallas_call | solution.py:261
  41.7 1.4 %copy.7 = f32[128,1,56]{0,2,1:T(8,128)} copy(f32[128,1,56]{0,2,1:T(8,128)} %bitcast.3) | data formatting | bytes 57344

commit v3 on v2

--- a/solution.py
+++ b/solution.py
@@ -116,15 +116,20 @@
             strided = slot[pl.ds(m, rows, stride=mats), :]
             summed += jnp.where(column_mat == m, strided, 0.0)
         source = chunk * held + lax.broadcasted_iota(jnp.int32, (held * mats, columns), 0) // mats
-        pick = jnp.where(source == order_ref[...], 1.0, 0.0).T
+        pick = jnp.where(source == order_ref[...], 1.0, 0.0).T.astype(jnp.bfloat16)
+        high = summed.astype(jnp.bfloat16)
+        rest = summed - high.astype(jnp.float32)
+        middle = rest.astype(jnp.bfloat16)
+        low = (rest - middle.astype(jnp.float32)).astype(jnp.bfloat16)
         for j in range(mat_count):
-            moved = lax.dot_general(
-                pick,
-                summed[j * quarter : (j + 1) * quarter],
-                (((1,), (1,)), ((), ())),
-                precision=lax.Precision.HIGHEST,
-                preferred_element_type=jnp.float32,
-            )
+            moved = jnp.zeros((columns, quarter), jnp.float32)
+            for part in (low, middle, high):
+                moved += lax.dot_general(
+                    pick,
+                    part[j * quarter : (j + 1) * quarter],
+                    (((1,), (1,)), ((), ())),
+                    preferred_element_type=jnp.float32,
+                )
             if first:
                 outgoing[j] = moved
             else:

time: 43.2 us -> 43.1 us (level)
  no operation moved by 1% of the time
where the time goes in v3:
time: 43.1 us; the launch traced here: 42.9 us
  Pallas kernels  40.9 us (95%)
  local copies, waits for them, and re-layouts  1.36 us (3%)
  between operations  0.66 us (2%)
    pallas_call x1, Pallas kernels, shards(): pl.pallas_call(functools.partial(kernel, n, mat_count, pieces), out_shape...  40.9 us
    unnamed x1, local copies, waits for them, and re-layouts  1.36 us

profile of v3, /device:TPU:0, one launch (start us, length us, event | category | flops | bytes accessed | tf_op | source)
XLA Modules:
  0.0 42.9 jit_solution(10312319716202804619)
XLA Ops:
  0.7 40.9 %shard_map.46 = f32[56,128]{1,0:T(8,128)} custom-call(bf16[256,4,4096]{2,1,0:T(4,128)(2,1)} %train_ref.1, bf16[1,14,4,4096]{3,2,1,0:T(4,128)(2,1)} %test_ref.1, s32[1]{0:T(128)S(6)} %copy.6.count_ref, s32[1,56]{1,0:T(1,128)} %order_ref.1), custom_call_target="tpu_custom_call" | custom-call | tf_op jit(solution)/shard_map/pallas_call | solution.py:266
  41.5 1.4 %copy.7 = f32[128,1,56]{0,2,1:T(8,128)} copy(f32[128,1,56]{0,2,1:T(8,128)} %bitcast.3) | data formatting | bytes 57344
